TPU v7x, 512 devices: a whole 4x4x16 slice. The times are simulated.
512 devices in a mesh: group: 16 (over z_lo, x), fsdp: 32 (over y, z_hi, core).
Axes of the slice: x: 4, y: 4, z: 16 (z_hi: 4, z_lo: 4; z = z_hi * 4 + z_lo), core: 2. Of those that a mesh axis runs over, the one named last changes fastest.
Arguments:
- hidden: bfloat16 [24576, 4608], P(('group', 'fsdp')), may hold values from -20 to 20
- down_w: bfloat16 [16, 2304, 4608], P('group', 'fsdp'), may hold values from -20 to 20
- moment_one: bfloat16 [16, 2304, 4608], P('group', 'fsdp'), may hold values from -0.75 to 0.75
- moment_two: bfloat16 [16, 2304, 4608], P('group', 'fsdp'), may hold values from 0.0049743652 to 0.049804688
- norm_gain: bfloat16 [2304], replicated, may hold values from 0.099609375 to 1.8984375
- cotangent: bfloat16 [24576, 2304], P(('group', 'fsdp')), may hold values from -6 to 6
- frag_delta: bfloat16 [16, 2304, 1024], P('group', 'fsdp'), may hold values from -6 to 6
- outer_params: float32 [2304, 1024], P('fsdp'), may hold values from -6 to 6
- outer_momentum: float32 [2304, 1024], P('fsdp'), may hold values from -6 to 6
Outputs:
- normed: bfloat16 [24576, 2304], P(('group', 'fsdp'))
- adam_step: bfloat16 [16, 2304, 4608], P('group', 'fsdp')
- new_outer: float32 [2304, 1024], P('fsdp')
All inputs are finite; a program needn't handle non-finite values.
Results may differ from a plain program's by a relative error of at most 0.0065.
Values may be sent and summed in bfloat16 or wider, within the bound.
A program may use at most 64 MiB of HBM per device.

v0:
```python
import jax
import jax.numpy as jnp
from jax import lax
from jax.sharding import PartitionSpec as P


def per_device(
    hidden,
    down_w,
    moment_one,
    moment_two,
    norm_gain,
    cotangent,
    frag_delta,
    outer_params,
    outer_momentum,
):
    gain = norm_gain.astype(jnp.float32)
    weight = down_w[0]
    total = lax.psum(frag_delta[0].astype(jnp.float32).astype(jnp.bfloat16), "group").astype(
        jnp.float32
    )
    average = total / lax.axis_size("group")
    momentum = 0.9 * outer_momentum + average
    new_outer = outer_params - 0.7 * (average + 0.9 * momentum)
    gathered = lax.all_gather(hidden, "fsdp", axis=0, tiled=True)
    columns = lax.dot_general(
        gathered, weight, (((1,), (1,)), ((), ())), preferred_element_type=jnp.float32
    ).astype(jnp.bfloat16)
    y_rows = lax.all_to_all(columns, "fsdp", split_axis=0, concat_axis=1, tiled=True)
    y_f = y_rows.astype(jnp.float32)
    scale = lax.rsqrt(jnp.mean(y_f * y_f, axis=1, keepdims=True) + 1e-06)
    normed = (y_f * scale * gain).astype(jnp.bfloat16)
    weighted = gain * cotangent.astype(jnp.float32)
    cross = jnp.mean(y_f * weighted, axis=1, keepdims=True)
    d_rows = (scale * (weighted - y_f * scale * scale * cross)).astype(jnp.bfloat16)
    d_cols = lax.all_to_all(d_rows, "fsdp", split_axis=1, concat_axis=0, tiled=True)
    grad = lax.dot_general(
        d_cols, gathered, (((0,), (0,)), ((), ())), preferred_element_type=jnp.float32
    )
    first_new = 0.9 * moment_one[0].astype(jnp.float32) + 0.1 * grad
    second_new = 0.95 * moment_two[0].astype(jnp.float32) + 0.05 * grad * grad
    step = first_new / (jnp.sqrt(second_new) + 1e-08) + 0.1 * weight.astype(jnp.float32)
    return (normed, step.astype(jnp.bfloat16)[None], new_outer)


def solution(mesh):
    placed = (
        P(("group", "fsdp"), None),
        P("group", "fsdp", None),
        P("group", "fsdp", None),
        P("group", "fsdp", None),
        P(),
        P(("group", "fsdp"), None),
        P("group", "fsdp", None),
        P("fsdp", None),
        P("fsdp", None),
    )
    return jax.shard_map(
        per_device,
        mesh=mesh,
        in_specs=placed,
        out_specs=(P(("group", "fsdp"), None), P("group", "fsdp", None), P("fsdp", None)),
        check_vma=False,
    )
```

profile of v0, /device:TPU:1, one launch (start us, length us, event | category | flops | bytes accessed | tf_op | source)
XLA Modules:
  0.0 437.6 jit_solution(17234807503369635539)
XLA Ops:
  8.0 0.0 all-gather.2.cloned.1.call-start
  8.0 0.7 all-gather.2.cloned.1.call-update
  8.7 204.9 %all-gather.2.cloned.1.call-done = bf16[1536,4608]{1,0:T(8,128)(2,1)} async-done(((bf16[48,4608]{1,0:T(8,128)(2,1)}), bf16[1536,4608]{1,0:T(8,128)(2,1)}) %all-gather.2.cloned.1.call-update) | async-done | bytes 14155792 | tf_op jit(solution)/shard_map/all_gather | solution.py:26
  213.7 9.5 %convolution_convert_fusion = bf16[1536,72]{0,1:T(8,128)(2,1)S(1)} fusion(bf16[1536,4608]{1,0:T(8,128)(2,1)} %all-gather.2.cloned.1.call-done, bf16[1,72,4608]{2,1,0:T(8,128)(2,1)} %param.10), kind=kOutput, calls=%fused_computation | convolution fusion | flops 1019326464 | bytes 15040512 | tf_op jit(solution)/shard_map/dot_general | solution.py:27
  223.1 0.0 copy-start.6
  223.1 0.9 copy.15
  224.1 10.3 %all-to-all-start = ((bf16[32,48,72]{2,1,0:T(8,128)(2,1)}), bf16[32,48,72]{2,1,0:T(8,128)(2,1)S(1)}, u32[]{:S(2)}, u32[]{:S(2)}) async-start(bf16[32,48,72]{2,1,0:T(8,128)(2,1)} %bitcast.1), calls=%async_computation | async-start | bytes 786432 | tf_op jit(solution)/shard_map/all_to_all | solution.py:30
  234.4 0.0 copy-done.6
  234.4 22.0 %all-to-all-done = bf16[32,48,72]{2,1,0:T(8,128)(2,1)S(1)} async-done(((bf16[32,48,72]{2,1,0:T(8,128)(2,1)}), bf16[32,48,72]{2,1,0:T(8,128)(2,1)S(1)}, u32[]{:S(2)}, u32[]{:S(2)}) %all-to-all-start) | async-done | bytes 221216 | tf_op jit(solution)/shard_map/all_to_all | solution.py:30
  256.3 0.1 convert_bitcast_fusion
  256.4 0.0 copy-start.1
  256.4 0.3 copy.16
  256.7 0.4 reshape.33
  257.1 0.2 copy-done.1
  257.3 0.2 multiply_reduce_fusion
  257.5 0.2 fusion.6
  257.7 0.9 multiply_convert_fusion
  258.6 0.0 copy-start.4
  258.6 0.0 copy-start.5
  258.6 0.9 all_to_all.26
  259.5 0.0 copy-start
  259.5 0.0 copy-start.2
  259.5 0.0 copy-start.3
  259.5 0.9 copy.17
  260.4 7.5 %all-to-all-start.1 = ((bf16[48,32,72]{2,0,1:T(8,128)(2,1)}), bf16[48,32,72]{2,0,1:T(8,128)(2,1)S(1)}, u32[]{:S(2)}, u32[]{:S(2)}) async-start(bf16[48,32,72]{2,0,1:T(8,128)(2,1)} %copy.17), calls=%async_computation.1 | async-start | bytes 786432 | tf_op jit(solution)/shard_map/all_to_all | solution.py:37
  267.9 0.0 all-reduce.2.cloned.1.call-start
  268.0 0.5 all-reduce.2.cloned.1.call-update
  268.5 150.7 %all-reduce.2.cloned.1.call-done = bf16[72,1024]{1,0:T(8,128)(2,1)} async-done(((bf16[72,1024]{1,0:T(8,128)(2,1)}), bf16[72,1024]{1,0:T(8,128)(2,1)}) %all-reduce.2.cloned.1.call-update) | async-done | bytes 147472 | tf_op jit(solution)/shard_map/psum | solution.py:20
  419.2 0.0 copy-done.4
  419.2 0.0 copy-done.5
  419.2 1.7 multiply_subtract_fusion
  421.0 0.0 all-to-all-done.1
  421.0 0.0 copy-done
  421.0 0.0 copy-done.2
  421.0 0.0 copy-done.3
  421.0 9.2 %fusion.8 = bf16[1,72,4608]{2,1,0:T(8,128)(2,1)} fusion(bf16[1,72,4608]{2,1,0:T(8,128)(2,1)S(1)} %copy-done, bf16[1,72,4608]{2,1,0:T(8,128)(2,1)S(1)} %copy-done.2, bf16[1,72,4608]{2,1,0:T(8,128)(2,1)S(1)} %copy-done.3, bf16[1536,72]{1,0:T(8,128)(2,1)S(1)} %bitcast.32, bf16[1536,4608]{1,0:T(8,128)(2,1)} %all-gather.2.cloned.1.call-done), kind=kOutput, calls=%fused_computation.13 | convolution fusion | flops 1024192512 | bytes 17031168 | tf_op jit(solution)/shard_map/dot_general | solution.py:38
  (2 shorter events, 0.0 us)
Async XLA Ops:
  8.0 205.7 %all-gather.2.cloned.1.call-start = ((), (), s32[]{:S(2)}) async-start(), calls=%async_computation.2 | async-start | bytes 14598144 | tf_op jit(solution)/shard_map/all_gather | solution.py:26
  223.1 11.2 %copy-start.6 = (bf16[2304]{0:T(1024)(128)(2,1)S(1)}, bf16[2304]{0:T(1024)(128)(2,1)}, u32[]{:S(2)}) copy-start(bf16[2304]{0:T(1024)(128)(2,1)} %param.13) | copy-start | bytes 13828
  224.1 32.3 %all-to-all-start = ((bf16[32,48,72]{2,1,0:T(8,128)(2,1)}), bf16[32,48,72]{2,1,0:T(8,128)(2,1)S(1)}, u32[]{:S(2)}, u32[]{:S(2)}) async-start(bf16[32,48,72]{2,1,0:T(8,128)(2,1)} %bitcast.1), calls=%async_computation | async-start | bytes 786432 | tf_op jit(solution)/shard_map/all_to_all | solution.py:30
  256.4 0.9 copy-start.1
  258.6 160.6 %copy-start.4 = (f32[72,1024]{1,0:T(8,128)S(1)}, f32[72,1024]{1,0:T(8,128)}, u32[]{:S(2)}) copy-start(f32[72,1024]{1,0:T(8,128)} %param.16) | copy-start | bytes 884740
  258.6 160.6 %copy-start.5 = (f32[72,1024]{1,0:T(8,128)S(1)}, f32[72,1024]{1,0:T(8,128)}, u32[]{:S(2)}) copy-start(f32[72,1024]{1,0:T(8,128)} %param.17) | copy-start | bytes 884740
  259.5 161.5 %copy-start = (bf16[1,72,4608]{2,1,0:T(8,128)(2,1)S(1)}, bf16[1,72,4608]{2,1,0:T(8,128)(2,1)}, u32[]{:S(2)}) copy-start(bf16[1,72,4608]{2,1,0:T(8,128)(2,1)} %param.10) | copy-start | bytes 1990660
  259.5 161.5 %copy-start.2 = (bf16[1,72,4608]{2,1,0:T(8,128)(2,1)S(1)}, bf16[1,72,4608]{2,1,0:T(8,128)(2,1)}, u32[]{:S(2)}) copy-start(bf16[1,72,4608]{2,1,0:T(8,128)(2,1)} %param.12) | copy-start | bytes 1990660
  259.5 161.4 %copy-start.3 = (bf16[1,72,4608]{2,1,0:T(8,128)(2,1)S(1)}, bf16[1,72,4608]{2,1,0:T(8,128)(2,1)}, u32[]{:S(2)}) copy-start(bf16[1,72,4608]{2,1,0:T(8,128)(2,1)} %param.11) | copy-start | bytes 1990660
  260.4 160.5 %all-to-all-start.1 = ((bf16[48,32,72]{2,0,1:T(8,128)(2,1)}), bf16[48,32,72]{2,0,1:T(8,128)(2,1)S(1)}, u32[]{:S(2)}, u32[]{:S(2)}) async-start(bf16[48,32,72]{2,0,1:T(8,128)(2,1)} %copy.17), calls=%async_computation.1 | async-start | bytes 786432 | tf_op jit(solution)/shard_map/all_to_all | solution.py:37
  267.9 151.3 %all-reduce.2.cloned.1.call-start = ((), (), s32[]{:S(2)}) async-start(), calls=%async_computation.3 | async-start | bytes 294912 | tf_op jit(solution)/shard_map/psum | solution.py:20
Sparse Core Ops, SparseCore 0:
  12.0 201.6 all-gather.1
Sparse Core Ops, SparseCore 1:
  271.3 147.9 all-reduce.1
where the time goes:
time: 446 us; the launch traced here: 438 us
  waiting for transfers between devices  379 us (85%)
  matrix products  18.6 us (4%)
  starting transfers between devices  17.9 us (4%)
  between operations  15.6 us (3%)
    all_gather x1, waiting for transfers between devices, per_device(): gathered = lax.all_gather(hidden, 'fsdp', axis=0, tiled=True)  205 us
    psum x1, waiting for transfers between devices, per_device(): lax.psum(frag_delta[0].astype(jnp.float32).astype(jnp.bfloat16), 'group')  151 us
    all_to_all x1, waiting for transfers between devices, per_device(): lax.all_to_all(columns, 'fsdp', split_axis=0, concat_axis=1, tiled=True)  22 us
    all_to_all x1, starting transfers between devices, per_device(): lax.all_to_all(columns, 'fsdp', split_axis=0, concat_axis=1, tiled=True)  10.3 us
    dot_general x1, matrix products, per_device(): lax.dot_general(gathered, weight, (((1,), (1,)), ((), ())), preferred_ele...  9.47 us
    dot_general x1, matrix products, per_device(): lax.dot_general(d_cols, gathered, (((0,), (0,)), ((), ())), preferred_ele...  9.15 us
  transfers between devices with their start and end apart: 4, of which 3 were waited for; matrix products, arithmetic and copies ran while one was open for 0% of the time, Pallas kernels for 0%

commit v1 on v0

v1 whole, which is shorter than its diff:
```python
import jax
import jax.numpy as jnp
from jax import lax
from jax.experimental import pallas as pl
from jax.experimental.pallas import tpu as pltpu
from jax.sharding import PartitionSpec as P

MESH = pl.DeviceIdType.MESH
F32 = jnp.float32
BF16 = jnp.bfloat16
D = 2304
HID = 4608
HALF = HID // 2
ROWS = 72
FEAT = 2 * ROWS
PAD = 80
PH = 3
TK = 256
CH = 1152
NCH = HID // CH


def body(
    h_in, w_in, m1_in, m2_in, gain_in, cot_in, delta_in, op_in, om_in,
    norm_out, adam_out, outer_out,
    hs, wp, w_own, m1, m2, grad, grad_in,
    cot_send, cot_recv, gain_rows, st_send, st_recv, a_keep, y_keep, ext_keep,
    ym_send, ym_recv, ye_send, ye_recv,
    d_own, d_recv, z_send, z_recv, o_own, o_recv, op, om,
    loc, zs_s, zs_r, zx_s, zx_r, ys_s, ys_r, yx_s, yx_r,
    w_s, w_r, cot_s, cot_r, st_s, st_r, ym_s, ym_r, ye_s, ye_r, g_s, g_r,
    dx_s, dx_r, dz_s, dz_r, do_s, do_r,
):
    g = lax.axis_index("group")
    f = lax.axis_index("fsdp")
    x, zl = lax.rem(g, 4), g // 4
    y, w, c = f // 8, lax.rem(f // 2, 4), lax.rem(f, 2)

    def dev(yy, ww, cc=None):
        return (g, yy * 8 + ww * 2 + (c if cc is None else cc))

    def far(xx, zz):
        return (zz * 4 + xx, f)

    def mod4(v):
        return lax.rem(v + 4, 4)

    def peer(o):
        return mod4(y + o // 4), mod4(w + lax.rem(o, 4))

    def rows16(s):
        return pl.ds(pl.multiple_of(s * 16, 16), 16)

    me = w * 4 + y
    mj = y * 4 + w
    yp, ym, wn, wm, wo = mod4(y + 1), mod4(y - 1), mod4(w + 1), mod4(w - 1), mod4(w + 2)
    yo = mod4(y + 2)

    sent = []

    def send(src, dst, s_sem, r_sem, where):
        cp = pltpu.make_async_remote_copy(
            src_ref=src, dst_ref=dst, send_sem=s_sem, recv_sem=r_sem,
            device_id=where, device_id_type=MESH,
        )
        cp.start()
        sent.append(cp)

    def arrived(dst, s_sem, r_sem, where):
        pltpu.make_async_remote_copy(
            src_ref=dst, dst_ref=dst, send_sem=s_sem, recv_sem=r_sem,
            device_id=where, device_id_type=MESH,
        ).wait_recv()

    barrier = pltpu.get_barrier_semaphore()

    @pl.loop(1, 16)
    def _(o):
        pl.semaphore_signal(barrier, inc=1, device_id=dev(*peer(o)), device_id_type=MESH)

    pl.semaphore_signal(barrier, inc=1, device_id=dev(y, w, 1 - c), device_id_type=MESH)
    for k in range(1, 4):
        pl.semaphore_signal(barrier, inc=1, device_id=far(mod4(x + k), zl), device_id_type=MESH)
        pl.semaphore_signal(barrier, inc=1, device_id=far(x, mod4(zl + k)), device_id_type=MESH)

    local = [
        pltpu.make_async_copy(h_in.at[pl.ds(16 * p, 16)], hs.at[p, rows16(me)], loc.at[p])
        for p in range(PH)
    ]
    local += [
        pltpu.make_async_copy(w_in, w_own, loc.at[3]),
        pltpu.make_async_copy(m1_in, m1, loc.at[4]),
        pltpu.make_async_copy(m2_in, m2, loc.at[5]),
        pltpu.make_async_copy(op_in, op, loc.at[6]),
        pltpu.make_async_copy(om_in, om, loc.at[7]),
    ]
    for cp in local:
        cp.start()

    zero = jnp.zeros((16, 80), F32)
    for j in range(16):
        part = cot_in[:, FEAT * j : FEAT * (j + 1)].astype(F32)
        tail = part[:, 128:]
        tail = jnp.concatenate([tail[0:16], tail[16:32], tail[32:48], zero], axis=1)
        cot_send[j] = jnp.concatenate([part[:, :128], tail], axis=0).astype(BF16)
        gj = gain_in[:, FEAT * j : FEAT * (j + 1)].astype(F32)
        gain_rows[j, 0:1, :] = gj[:, :128]
        gain_rows[j, 1:2, :] = jnp.concatenate([gj[:, 128:], jnp.zeros((1, 112), F32)], axis=1)
    delta = delta_in[...].astype(F32)
    for k in range(4):
        d_own[k] = delta[:, 256 * k : 256 * (k + 1)]
    local[3].wait()
    w32 = w_own[...].astype(F32)
    wp[c] = jnp.concatenate([w32, jnp.zeros((PAD - ROWS, HID), F32)], axis=0).astype(BF16)

    pl.semaphore_wait(barrier, 22)

    def own(p):
        src = h_in.at[pl.ds(16 * p, 16)]
        dst = hs.at[p, rows16(me)]
        send(src, dst, zs_s.at[p, 0], zs_r.at[p, 0], dev(y, wn))
        send(src, dst, zs_s.at[p, 1], zs_r.at[p, 1], dev(y, wm))
        spread(p, 0, src)

    def spread(p, q, src=None):
        slot = (w, wm, wn, wo)[q] * 4 + y
        dst = hs.at[p, rows16(slot)]
        src = dst if src is None else src
        send(src, dst, ys_s.at[p, q, 0], ys_r.at[p, q, 0], dev(yp, w))
        send(src, dst, ys_s.at[p, q, 1], ys_r.at[p, q, 1], dev(ym, w))

    def half(k):
        return pl.ds(k * HALF, HALF)

    def relay_z(p):
        for k, (came, to) in enumerate(((wm, wn), (wn, wm))):
            blk = hs.at[p, rows16(came * 4 + y)]
            arrived(blk, zs_s.at[p, k], zs_r.at[p, k], dev(y, to))
            part = hs.at[p, rows16(came * 4 + y), half(k)]
            send(part, part, zx_s.at[p, k], zx_r.at[p, k], dev(y, to))

    def got_z(p):
        for k, to in enumerate((wn, wm)):
            part = hs.at[p, rows16(wo * 4 + y), half(k)]
            arrived(part, zx_s.at[p, k], zx_r.at[p, k], dev(y, to))

    def relay_y(p, q):
        ww = (w, wm, wn, wo)[q]
        for k, (came, to) in enumerate(((ym, yp), (yp, ym))):
            blk = hs.at[p, rows16(ww * 4 + came)]
            arrived(blk, ys_s.at[p, q, k], ys_r.at[p, q, k], dev(to, w))
            part = hs.at[p, rows16(ww * 4 + came), half(k)]
            send(part, part, yx_s.at[p, q, k], yx_r.at[p, q, k], dev(to, w))

    def got_y(p):
        for q, ww in enumerate((w, wm, wn, wo)):
            for k, to in enumerate((yp, ym)):
                part = hs.at[p, rows16(ww * 4 + yo), half(k)]
                arrived(part, yx_s.at[p, q, k], yx_r.at[p, q, k], dev(to, w))

    own(0)
    send(wp.at[c], wp.at[c], w_s.at[0], w_r.at[0], dev(y, w, 1 - c))

    def cot_copy(o):
        yy, ww = peer(o)
        return pltpu.make_async_remote_copy(
            src_ref=cot_send.at[yy * 4 + ww], dst_ref=cot_recv.at[me],
            send_sem=cot_s.at[o], recv_sem=cot_r.at[me],
            device_id=dev(yy, ww), device_id_type=MESH,
        )

    @pl.loop(1, 16)
    def _(o):
        cot_copy(o).start()

    for k in range(1, 4):
        xx = mod4(x + k)
        send(d_own.at[xx], d_recv.at[x], dx_s.at[k], dx_r.at[x], far(xx, zl))
    own(1)
    cot_recv[me] = cot_send[mj]
    d_recv[x] = d_own[x]

    relay_z(0)
    spread(0, 1)
    spread(0, 2)
    relay_y(0, 0)
    own(2)
    relay_y(0, 1)
    relay_y(0, 2)

    for k in range(1, 4):
        xx = mod4(x + k)
        arrived(d_recv.at[xx], dx_s.at[k], dx_r.at[xx], far(xx, zl))
    part_x = d_recv[0] + d_recv[1] + d_recv[2] + d_recv[3]
    z_send[...] = jnp.concatenate([part_x, jnp.zeros((PAD - ROWS, 256), F32)], axis=0).astype(BF16)
    z_recv[zl] = z_send[...]
    for k in range(1, 4):
        zz = mod4(zl + k)
        send(z_send, z_recv.at[zl], dz_s.at[k], dz_r.at[zl], far(x, zz))

    got_z(0)
    spread(0, 3)

    arrived(wp.at[1 - c], w_s.at[0], w_r.at[0], dev(y, w, 1 - c))

    @pl.loop(1, 16)
    def _(o):
        yy, ww = peer(o)
        arrived(cot_recv.at[ww * 4 + yy], cot_s.at[o], cot_r.at[ww * 4 + yy], dev(yy, ww))

    gt = gain_rows[mj]
    gmain = jnp.broadcast_to(gt[0:1, :], (128, 128)).T
    gext = jnp.broadcast_to(gt[1:2, :], (128, 128)).T
    gcol = jnp.concatenate([gmain, gext[0:16]], axis=0)
    gcol = jnp.concatenate([gcol, gcol], axis=1)
    ext_all = cot_recv[:, 48:64, :].reshape(TK, 128).astype(F32).T
    for p in range(PH):
        main = cot_recv[:, 16 * p : 16 * p + 16, :].reshape(TK, 128).astype(F32).T
        a_keep[p] = gcol * jnp.concatenate([main, ext_all[16 * p : 16 * p + 16]], axis=0)
    local[0].wait()
    local[1].wait()
    local[2].wait()

    def st_copy(p, o):
        yy, ww = peer(o)
        return pltpu.make_async_remote_copy(
            src_ref=st_send.at[p], dst_ref=st_recv.at[p, mj],
            send_sem=st_s.at[p, o], recv_sem=st_r.at[p, mj],
            device_id=dev(yy, ww), device_id_type=MESH,
        )

    def ym_copy(p, o):
        yy, ww = peer(o)
        return pltpu.make_async_remote_copy(
            src_ref=ym_send.at[p, ww * 4 + yy], dst_ref=ym_recv.at[p, mj],
            send_sem=ym_s.at[p, o], recv_sem=ym_r.at[p, mj],
            device_id=dev(yy, ww), device_id_type=MESH,
        )

    def ye_copy(o):
        yy, ww = peer(o)
        return pltpu.make_async_remote_copy(
            src_ref=ye_send.at[ww * 4 + yy], dst_ref=ye_recv.at[mj],
            send_sem=ye_s.at[o], recv_sem=ye_r.at[mj],
            device_id=dev(yy, ww), device_id_type=MESH,
        )

    def project(p):
        got_y(p)
        prod = lax.dot_general(
            wp[...].reshape(2 * PAD, HID), hs[p], (((1,), (1,)), ((), ())),
            preferred_element_type=F32,
        )
        val = jnp.concatenate([prod[0:ROWS], prod[PAD : PAD + ROWS]], axis=0)
        val = val.astype(BF16).astype(F32)
        y_keep[p] = val
        square = jnp.sum(val * val, axis=0, keepdims=True)
        cross = jnp.sum(val * a_keep[p], axis=0, keepdims=True)
        both = jnp.concatenate([square, cross], axis=0)
        st_send[p] = both
        st_recv[p, mj] = both

        @pl.loop(1, 16)
        def _(o):
            st_copy(p, o).start()

        ym_send[p] = val[0:128].T.astype(BF16).reshape(16, 16, 128)
        ext_keep[16 * p : 16 * p + 16, :] = val[128:144]
        ym_recv[p, mj] = ym_send[p, me]

        @pl.loop(1, 16)
        def _(o):
            ym_copy(p, o).start()

    def weights(p, last=False):
        @pl.loop(1, 16)
        def _(o):
            yy, ww = peer(o)
            j = yy * 4 + ww
            arrived(st_recv.at[p, j], st_s.at[p, o], st_r.at[p, j], dev(yy, ww))

        tot = jnp.sum(st_recv[p], axis=0)
        scale = lax.rsqrt(tot[0:1] / D + 1e-06)
        cross = tot[1:2] / D
        dy = (scale * (a_keep[p] - y_keep[p] * (scale * scale * cross))).astype(BF16)
        for k in range(NCH):
            cols = pl.ds(k * CH, CH)
            add = jnp.dot(dy, hs[p, :, cols], preferred_element_type=F32)
            if p == 0:
                grad[:, cols] = add
            else:
                grad[:, cols] += add
            if last:
                other = pl.ds(pl.multiple_of((1 - c) * ROWS, 8), ROWS)
                send(grad.at[other, cols], grad_in.at[:, cols], g_s.at[k], g_r.at[k], dev(y, w, 1 - c))

    relay_z(1)
    spread(1, 1)
    spread(1, 2)
    relay_y(1, 0)
    relay_y(0, 3)
    relay_y(1, 1)
    relay_y(1, 2)
    project(0)

    for k in range(1, 4):
        zz = mod4(zl + k)
        arrived(z_recv.at[zz], dz_s.at[k], dz_r.at[zz], far(x, zz))
    total = z_recv[0].astype(F32) + z_recv[1].astype(F32) + z_recv[2].astype(F32) + z_recv[3].astype(F32)
    o_own[...] = total[0:ROWS]
    o_recv[x] = o_own[...]
    for k in range(1, 4):
        xx = mod4(x + k)
        send(o_own, o_recv.at[x], do_s.at[k], do_r.at[x], far(xx, zl))

    got_z(1)
    spread(1, 3)
    relay_z(2)
    spread(2, 1)
    spread(2, 2)
    relay_y(2, 0)
    relay_y(1, 3)
    relay_y(2, 1)
    relay_y(2, 2)
    weights(0)
    project(1)

    for k in range(1, 4):
        xx = mod4(x + k)
        arrived(o_recv.at[xx], do_s.at[k], do_r.at[xx], far(xx, zl))
    local[6].wait()
    local[7].wait()
    for k in range(4):
        cols = slice(256 * k, 256 * (k + 1))
        average = o_recv[k] / 16.0
        momentum = 0.9 * om[:, cols] + average
        outer_out[:, cols] = op[:, cols] - 0.7 * (average + 0.9 * momentum)

    weights(1)
    got_z(2)
    spread(2, 3)
    relay_y(2, 3)
    project(2)
    ext = jnp.concatenate([ext_keep[...], jnp.zeros((80, TK), F32)], axis=0)
    ye_send[...] = ext.T.astype(BF16).reshape(16, 16, 128)
    ye_recv[mj] = ye_send[me]

    @pl.loop(1, 16)
    def _(o):
        ye_copy(o).start()

    weights(2, last=True)

    local[4].wait()
    local[5].wait()
    mine = pl.ds(pl.multiple_of(c * ROWS, 8), ROWS)
    for k in range(NCH):
        cols = pl.ds(k * CH, CH)
        arrived(grad_in.at[:, cols], g_s.at[k], g_r.at[k], dev(y, w, 1 - c))
        gr = grad[mine, cols] + grad_in[:, cols]
        first = 0.9 * m1[:, cols].astype(F32) + 0.1 * gr
        second = 0.95 * m2[:, cols].astype(F32) + 0.05 * gr * gr
        step = first / (jnp.sqrt(second) + 1e-08) + 0.1 * w_own[:, cols].astype(F32)
        adam_out[:, cols] = step.astype(BF16)

    @pl.loop(1, 16)
    def _(o):
        yy, ww = peer(o)
        j = yy * 4 + ww
        for p in range(PH):
            arrived(ym_recv.at[p, j], ym_s.at[p, o], ym_r.at[p, j], dev(yy, ww))
        arrived(ye_recv.at[j], ye_s.at[o], ye_r.at[j], dev(yy, ww))

    gain = gain_in[...].astype(F32)
    for p in range(PH):
        parts = []
        for j in range(16):
            parts.append(ym_recv[p, j].astype(F32))
            parts.append(ye_recv[j].astype(F32)[:, 16 * p : 16 * p + 16])
        val = jnp.concatenate(parts, axis=1)
        scale = lax.rsqrt(jnp.mean(val * val, axis=1, keepdims=True) + 1e-06)
        norm_out[16 * p : 16 * p + 16, :] = (val * scale * gain).astype(BF16)

    for cp in sent:
        cp.wait_send()

    @pl.loop(1, 16)
    def _(o):
        cot_copy(o).wait_send()
        for p in range(PH):
            st_copy(p, o).wait_send()
            ym_copy(p, o).wait_send()
        ye_copy(o).wait_send()


def per_device(hidden, down_w, m1, m2, gain, cot, delta, outer_params, outer_momentum):
    vm = pl.BlockSpec(memory_space=pltpu.VMEM)
    hbm = pl.BlockSpec(memory_space=pl.ANY)
    dma = pltpu.SemaphoreType.DMA
    scratch = [
        pltpu.VMEM((PH, TK, HID), BF16),
        pltpu.VMEM((2, PAD, HID), BF16),
        pltpu.VMEM((ROWS, HID), BF16),
        pltpu.VMEM((ROWS, HID), BF16),
        pltpu.VMEM((ROWS, HID), BF16),
        pltpu.VMEM((FEAT, HID), F32),
        pltpu.VMEM((ROWS, HID), F32),
        pltpu.VMEM((16, 64, 128), BF16),
        pltpu.VMEM((16, 64, 128), BF16),
        pltpu.VMEM((16, 8, 128), F32),
        pltpu.VMEM((PH, 2, TK), F32),
        pltpu.VMEM((PH, 16, 2, TK), F32),
        pltpu.VMEM((PH, FEAT, TK), F32),
        pltpu.VMEM((PH, FEAT, TK), F32),
        pltpu.VMEM((48, TK), F32),
        pltpu.VMEM((PH, 16, 16, 128), BF16),
        pltpu.VMEM((PH, 16, 16, 128), BF16),
        pltpu.VMEM((16, 16, 128), BF16),
        pltpu.VMEM((16, 16, 128), BF16),
        pltpu.VMEM((4, ROWS, 256), F32),
        pltpu.VMEM((4, ROWS, 256), F32),
        pltpu.VMEM((PAD, 256), BF16),
        pltpu.VMEM((4, PAD, 256), BF16),
        pltpu.VMEM((ROWS, 256), F32),
        pltpu.VMEM((4, ROWS, 256), F32),
        pltpu.VMEM((ROWS, 1024), F32),
        pltpu.VMEM((ROWS, 1024), F32),
        dma((8,)),
        dma((PH, 2)), dma((PH, 2)), dma((PH, 2)), dma((PH, 2)),
        dma((PH, 4, 2)), dma((PH, 4, 2)), dma((PH, 4, 2)), dma((PH, 4, 2)),
        dma((1,)), dma((1,)),
        dma((16,)), dma((16,)),
        dma((PH, 16)), dma((PH, 16)),
        dma((PH, 16)), dma((PH, 16)),
        dma((16,)), dma((16,)),
        dma((NCH,)), dma((NCH,)),
        dma((4,)), dma((4,)), dma((4,)), dma((4,)), dma((4,)), dma((4,)),
    ]
    normed, adam, outer = pl.pallas_call(
        body,
        out_shape=(
            jax.ShapeDtypeStruct((48, D), BF16),
            jax.ShapeDtypeStruct((ROWS, HID), BF16),
            jax.ShapeDtypeStruct((ROWS, 1024), F32),
        ),
        in_specs=[hbm, hbm, hbm, hbm, vm, vm, vm, hbm, hbm],
        out_specs=(vm, vm, vm),
        scratch_shapes=scratch,
        compiler_params=pltpu.CompilerParams(
            collective_id=0, has_side_effects=True, vmem_limit_bytes=50 << 20
        ),
        cost_estimate=pl.CostEstimate(flops=2 * 10**9, bytes_accessed=4 * 10**6, transcendentals=0),
    )(
        hidden, down_w[0], m1[0], m2[0], gain.reshape(1, D), cot, delta[0],
        outer_params, outer_momentum,
    )
    return normed, adam[None], outer


def solution(mesh):
    placed = (
        P(("group", "fsdp"), None),
        P("group", "fsdp", None),
        P("group", "fsdp", None),
        P("group", "fsdp", None),
        P(),
        P(("group", "fsdp"), None),
        P("group", "fsdp", None),
        P("fsdp", None),
        P("fsdp", None),
    )
    return jax.shard_map(
        per_device,
        mesh=mesh,
        in_specs=placed,
        out_specs=(P(("group", "fsdp"), None), P("group", "fsdp", None), P("fsdp", None)),
        check_vma=False,
    )
```

time: 446 us -> 150 us (0.34); the launches traced: 438 us -> 149 us
  waiting for transfers between devices: 379 us -> 0 us
  Pallas kernels: 0 us -> 138 us
  matrix products: 18.6 us -> 0 us
  starting transfers between devices: 17.9 us -> 0 us
  between operations: 15.6 us -> 0.66 us
  local copies, waits for them, and re-layouts: 3.66 us -> 9.88 us
    all_gather x1 -> x0, waiting for transfers between devices: 205 us -> none  [per_device(): gathered = lax.all_gather(hidden, 'fsdp', axis=0, tiled=True)]
    psum x1 -> x0, waiting for transfers between devices: 151 us -> none  [per_device(): lax.psum(frag_delta[0].astype(jnp.float32).astype(jnp.bfloat16), 'group')]
    pallas_call x0 -> x1, Pallas kernels: none -> 138 us  [per_device(): pl.pallas_call(body, out_shape=(jax.ShapeDtypeStruct((48, D), BF16), jax....]
    all_to_all x2 -> x0, waiting for transfers between devices: 22 us -> none  [the longest x1 22 us: per_device(): lax.all_to_all(columns, 'fsdp', split_axis=0, concat_axis=1, tiled=True)]
    dot_general x2 -> x0, matrix products: 18.6 us -> none  [the longest x1 9.47 us: per_device(): lax.dot_general(gathered, weight, (((1,), (1,)), ((), ())), preferred_ele...]
    all_to_all x2 -> x0, starting transfers between devices: 17.8 us -> none  [the longest x1 10.3 us: per_device(): lax.all_to_all(columns, 'fsdp', split_axis=0, concat_axis=1, tiled=True)]
    unnamed x14 -> x19, local copies, waits for them, and re-layouts: 0.27 us -> 9.88 us
  transfers between devices with their start and end apart: 4 -> 0, of which waited for: 3 -> 0; matrix products, arithmetic and copies ran while one was open for 0% -> 0% of each run, Pallas kernels for 0% -> 0%
where the time goes in v1:
time: 150 us; the launch traced here: 149 us
  Pallas kernels  138 us (92%)
  local copies, waits for them, and re-layouts  9.88 us (7%)
    pallas_call x1, Pallas kernels, per_device(): pl.pallas_call(body, out_shape=(jax.ShapeDtypeStruct((48, D), BF16), jax....  138 us
    unnamed x19, local copies, waits for them, and re-layouts  9.88 us

profile of v1, /device:TPU:1, one launch (start us, length us, event | category | flops | bytes accessed | tf_op | source)
XLA Modules:
  0.0 148.8 jit_solution(1064185993844162633)
XLA Ops:
  0.6 0.0 copy-start.7
  0.6 0.7 copy-done.7
  1.3 0.0 copy-start
  1.3 1.1 copy-done
  2.4 0.0 copy-start.1
  2.4 1.1 copy-done.1
  3.5 0.0 copy-start.2
  3.5 1.0 copy-done.2
  4.5 0.0 copy-start.3
  4.5 1.0 copy-done.3
  5.5 0.0 copy-start.4
  5.5 1.0 copy-done.4
  6.4 0.0 copy-start.5
  6.5 0.9 copy-done.5
  7.4 0.0 copy-start.6
  7.4 0.9 copy-done.6
  8.3 138.3 %shard_map.112 = (bf16[48,2304]{1,0:T(8,128)(2,1)S(1)}, bf16[72,4608]{1,0:T(8,128)(2,1)S(1)}, f32[72,1024]{1,0:T(8,128)S(1)}) custom-call(bf16[48,4608]{1,0:T(8,128)(2,1)S(1)} %copy-done.2, bf16[72,4608]{1,0:T(8,128)(2,1)S(1)} %bitcast.6, bf16[72,4608]{1,0:T(8,128)(2,1)S(1)} %bitcast.7, bf16[72,4608]{1,0:T(8,128)(2,1)} %bitcast.9, ...), custom_call_target="tpu_custom_call" | custom-call | flops 2000000000 | bytes 4000000 | tf_op jit(solution)/shard_map/pallas_call | solution.py:439
  146.6 0.7 copy.15
  147.3 0.8 copy.16
  148.1 0.7 copy.17
  (1 shorter events, 0.0 us)
Async XLA Ops:
  0.6 0.7 copy-start.7
  1.3 1.1 copy-start
  2.4 1.1 copy-start.1
  3.5 1.0 copy-start.2
  4.5 1.0 copy-start.3
  5.5 1.0 copy-start.4
  6.4 0.9 copy-start.5
  7.4 0.9 copy-start.6

commit v2 on v0

v2 whole, which is shorter than its diff:
```python
import jax
import jax.numpy as jnp
from jax import lax
from jax.experimental import pallas as pl
from jax.experimental.pallas import tpu as pltpu
from jax.sharding import PartitionSpec as P

MESH = pl.DeviceIdType.MESH
F32 = jnp.float32
BF16 = jnp.bfloat16
D = 2304
HID = 4608
HALF = HID // 2
ROWS = 72
FEAT = 2 * ROWS
PAD = 80
PH = 3
TK = 256
CH = 1152
NCH = HID // CH


def body(
    h_in, w_in, m1_in, m2_in, gain_in, cot_in, delta_in, op_in, om_in,
    norm_hbm, adam_hbm, outer_hbm,
    norm_out, adam_out, outer_out, gain_v,
    hs, wp, w_own, m1, m2, grad, grad_in, cot, delta,
    cot_send, cot_mid, cot_recv, gain_rows, sa_send, sa_recv, sb_send, sb_recv, a_keep, y_keep,
    ra_send, ra_recv, rb_send, rb_recv,
    d_own, d_recv, z_send, z_recv, o_own, o_recv, op, om,
    loc, out_sem, tok_s, zs_r, zx_r, ys_r, yh_r, yx_r,
    w_s, w_r, cot_s, cot_r, all_s, all_r, g_s, g_r,
    dx_s, dx_r, dz_s, dz_r, do_s, do_r,
):
    g = lax.axis_index("group")
    f = lax.axis_index("fsdp")
    x, zl = lax.rem(g, 4), g // 4
    y, w, c = f // 8, lax.rem(f // 2, 4), lax.rem(f, 2)

    def dev(yy, ww, cc=None):
        return (g, yy * 8 + ww * 2 + (c if cc is None else cc))

    def far(xx, zz):
        return (zz * 4 + xx, f)

    def mod4(v):
        return lax.rem(v + 4, 4)

    def peer(o):
        return mod4(y + o // 4), mod4(w + lax.rem(o, 4))

    def rows16(s):
        return pl.ds(pl.multiple_of(s * 16, 16), 16)

    me = w * 4 + y
    mj = y * 4 + w
    yp, ym, wn, wm, wo = mod4(y + 1), mod4(y - 1), mod4(w + 1), mod4(w - 1), mod4(w + 2)
    yo = mod4(y + 2)
    twin = dev(y, w, 1 - c)

    sent, written = [], []

    def put(src, dst, i):
        cp = pltpu.make_async_copy(src, dst, out_sem.at[i])
        cp.start()
        written.append(cp)

    def send(src, dst, s_sem, r_sem, where, keep=True):
        cp = pltpu.make_async_remote_copy(
            src_ref=src, dst_ref=dst, send_sem=s_sem, recv_sem=r_sem,
            device_id=where, device_id_type=MESH,
        )
        cp.start()
        if keep:
            sent.append(cp)

    def arrived(dst, sem):
        pltpu.make_async_copy(dst, dst, sem).wait()

    barrier = pltpu.get_barrier_semaphore()

    @pl.loop(1, 16)
    def _(o):
        pl.semaphore_signal(barrier, inc=1, device_id=dev(*peer(o)), device_id_type=MESH)

    pl.semaphore_signal(barrier, inc=1, device_id=twin, device_id_type=MESH)
    for k in range(1, 4):
        pl.semaphore_signal(barrier, inc=1, device_id=far(mod4(x + k), zl), device_id_type=MESH)
        pl.semaphore_signal(barrier, inc=1, device_id=far(x, mod4(zl + k)), device_id_type=MESH)

    local = [
        pltpu.make_async_copy(src, dst, loc.at[i])
        for i, (src, dst) in enumerate((
            (cot_in, cot), (delta_in, delta), (w_in, w_own),
            (h_in.at[pl.ds(0, 16)], hs.at[0, rows16(me)]),
            (h_in.at[pl.ds(16, 16)], hs.at[1, rows16(me)]),
            (h_in.at[pl.ds(32, 16)], hs.at[2, rows16(me)]),
            (m1_in, m1), (m2_in, m2), (op_in, op), (om_in, om), (gain_in, gain_v),
        ))
    ]
    for cp in local:
        cp.start()

    pl.semaphore_wait(barrier, 22)

    def half(k):
        return pl.ds(k * HALF, HALF)

    def own_z(p):
        src = h_in.at[pl.ds(16 * p, 16)]
        dst = hs.at[p, rows16(me)]
        send(src, dst, tok_s.at[p], zs_r.at[p, 0], dev(y, wn), False)
        send(src, dst, tok_s.at[p], zs_r.at[p, 1], dev(y, wm), False)

    def spread(p, q, src=None):
        dst = hs.at[p, rows16((w, wm, wn)[q] * 4 + y)]
        src = dst if src is None else src
        send(src, dst, tok_s.at[p], ys_r.at[p, q, 0], dev(yp, w), False)
        send(src, dst, tok_s.at[p], ys_r.at[p, q, 1], dev(ym, w), False)

    def relay_z(p):
        for k, (came, to) in enumerate(((wm, wn), (wn, wm))):
            arrived(hs.at[p, rows16(came * 4 + y)], zs_r.at[p, k])
            part = hs.at[p, rows16(came * 4 + y), half(k)]
            send(part, part, tok_s.at[p], zx_r.at[p, k], dev(y, to), False)

    def finish_z(p):
        for k in range(2):
            part = hs.at[p, rows16(wo * 4 + y), half(k)]
            arrived(part, zx_r.at[p, k])
            to, fro = ((yp, ym), (ym, yp))[k]
            send(part, part, tok_s.at[p], yh_r.at[p, k], dev(to, w), False)
            send(part, part, tok_s.at[p], yx_r.at[p], dev(fro, w), False)

    def relay_y(p, q):
        ww = (w, wm, wn)[q]
        for k, (came, to) in enumerate(((ym, yp), (yp, ym))):
            arrived(hs.at[p, rows16(ww * 4 + came)], ys_r.at[p, q, k])
            part = hs.at[p, rows16(ww * 4 + came), half(k)]
            send(part, part, tok_s.at[p], yx_r.at[p], dev(to, w), False)

    def relay_last(p):
        for k, (came, to) in enumerate(((ym, yp), (yp, ym))):
            part = hs.at[p, rows16(wo * 4 + came), half(k)]
            arrived(part, yh_r.at[p, k])
            send(part, part, tok_s.at[p], yx_r.at[p], dev(to, w), False)

    def got_y(p):
        arrived(hs.at[p, pl.ds(0, 80)], yx_r.at[p])

    def cot_y():
        for k in range(1, 4):
            yy = mod4(y + k)
            src = cot_send.at[pl.ds(pl.multiple_of(yy * 4, 4), 4)]
            send(src, cot_mid.at[y], cot_s.at[0], cot_r.at[0], dev(yy, w), False)
        cot_mid[y] = cot_send[pl.ds(pl.multiple_of(y * 4, 4), 4)]

    def cot_z():
        arrived(cot_mid.at[pl.ds(0, 3)], cot_r.at[0])
        here = pl.ds(pl.multiple_of(w * 4, 4), 4)
        for k in (1, 3, 2):
            ww = mod4(w + k)
            send(cot_mid.at[:, ww], cot_recv.at[here], cot_s.at[1], cot_r.at[1], dev(y, ww), False)
        cot_recv[here] = cot_mid[:, w]

    def outer_x():
        local[1].wait()
        d32 = delta[...].astype(F32)
        for k in range(4):
            d_own[k] = d32[:, 256 * k : 256 * (k + 1)]
        for k in range(1, 4):
            xx = mod4(x + k)
            send(d_own.at[xx], d_recv.at[x], dx_s.at[k], dx_r.at[x], far(xx, zl))
        d_recv[x] = d_own[x]

    def outer_z():
        for k in range(1, 4):
            xx = mod4(x + k)
            arrived(d_recv.at[xx], dx_r.at[xx])
        part_x = d_recv[0] + d_recv[1] + d_recv[2] + d_recv[3]
        z_send[...] = jnp.concatenate([part_x, jnp.zeros((PAD - ROWS, 256), F32)], axis=0).astype(BF16)
        z_recv[zl] = z_send[...]
        for k in range(1, 4):
            zz = mod4(zl + k)
            send(z_send, z_recv.at[zl], dz_s.at[k], dz_r.at[zl], far(x, zz))

    def outer_back():
        for k in range(1, 4):
            zz = mod4(zl + k)
            arrived(z_recv.at[zz], dz_r.at[zz])
        total = z_recv[0].astype(F32) + z_recv[1].astype(F32) + z_recv[2].astype(F32) + z_recv[3].astype(F32)
        o_own[...] = total[0:ROWS]
        o_recv[x] = o_own[...]
        for k in range(1, 4):
            xx = mod4(x + k)
            send(o_own, o_recv.at[x], do_s.at[k], do_r.at[x], far(xx, zl))

    def outer_step():
        for k in range(1, 4):
            xx = mod4(x + k)
            arrived(o_recv.at[xx], do_r.at[xx])
        local[8].wait()
        local[9].wait()
        for k in range(4):
            cols = slice(256 * k, 256 * (k + 1))
            average = o_recv[k] / 16.0
            momentum = 0.9 * om[:, cols] + average
            outer_out[:, cols] = op[:, cols] - 0.7 * (average + 0.9 * momentum)
        put(outer_out, outer_hbm, 0)

    def share_w():
        local[2].wait()
        w32 = w_own[...].astype(F32)
        wp[c] = jnp.concatenate([w32, jnp.zeros((PAD - ROWS, HID), F32)], axis=0).astype(BF16)
        send(wp.at[c], wp.at[c], w_s.at[0], w_r.at[0], twin)

    def pack_cot():
        zero = jnp.zeros((16, 80), F32)
        local[0].wait()
        local[10].wait()
        gain = gain_v[...].reshape(1, D).astype(F32)
        for j in range(16):
            part = cot[:, FEAT * j : FEAT * (j + 1)].astype(F32)
            tail = part[:, 128:]
            tail = jnp.concatenate([tail[0:16], tail[16:32], tail[32:48], zero], axis=1)
            cot_send[j] = jnp.concatenate([part[:, :128], tail], axis=0).astype(BF16)
            gj = gain[:, FEAT * j : FEAT * (j + 1)]
            gain_rows[j, 0:1, :] = gj[:, :128]
            gain_rows[j, 1:2, :] = jnp.concatenate([gj[:, 128:], jnp.zeros((1, 112), F32)], axis=1)

    def own(p):
        spread(p, 0, h_in.at[pl.ds(16 * p, 16)])

    def ready():
        arrived(wp.at[1 - c], w_r.at[0])
        local[3].wait()
        local[4].wait()
        local[5].wait()

    def get_cot():
        arrived(cot_recv.at[pl.ds(0, 12)], cot_r.at[1])

        gt = gain_rows[mj]
        gmain = jnp.broadcast_to(gt[0:1, :], (128, 128)).T
        gext = jnp.broadcast_to(gt[1:2, :], (128, 128)).T
        gcol = jnp.concatenate([gmain, gext[0:16]], axis=0)
        gcol = jnp.concatenate([gcol, gcol], axis=1)
        ext_all = cot_recv[:, 48:64, :].reshape(TK, 128).astype(F32).T
        for p in range(PH):
            main = cot_recv[:, 16 * p : 16 * p + 16, :].reshape(TK, 128).astype(F32).T
            a_keep[p] = gcol * jnp.concatenate([main, ext_all[16 * p : 16 * p + 16]], axis=0)

    def sums_a():
        both = jnp.concatenate([sums(0), sums(1)], axis=1)
        sa_send[...] = both
        sa_recv[mj] = both

    def sums_b():
        both = sums(2)
        sb_send[...] = both
        sb_recv[mj] = both

    def weights_a():
        got_all(sa_recv, 0)

        tot = jnp.sum(sa_recv[...], axis=0)
        weights(0, tot[:, 0:TK])
        weights(1, tot[:, TK : 2 * TK])

    def get_b():
        got_all(sb_recv, 1)

    def weights_b():
        weights(2, jnp.sum(sb_recv[...], axis=0), last=True)

    def swapped(k):
        cols = pl.ds(k * CH, CH)
        arrived(grad_in.at[:, cols], g_r.at[k])

    def adam(k):
        mine = pl.ds(pl.multiple_of(c * ROWS, 8), ROWS)
        cols = pl.ds(k * CH, CH)
        gr = grad[mine, cols] + grad_in[:, cols]
        first = 0.9 * m1[:, cols].astype(F32) + 0.1 * gr
        second = 0.95 * m2[:, cols].astype(F32) + 0.05 * gr * gr
        step = first / (jnp.sqrt(second) + 1e-08) + 0.1 * w_own[:, cols].astype(F32)
        adam_out[:, cols] = step.astype(BF16)
        put(adam_out.at[:, cols], adam_hbm.at[:, cols], 2 + k)

    def moments():
        local[6].wait()
        local[7].wait()

    def get_ret():
        got_all(ra_recv, 2)
        got_all(rb_recv, 3)

    def norm_rows():
        gain = gain_v[...].reshape(1, D).astype(F32)
        for p in range(PH):
            parts = []
            for j in range(16):
                main = ra_recv[j, 16 * p : 16 * p + 16, :] if p < 2 else rb_recv[j, 0:16, :]
                parts.append(main.astype(F32))
                parts.append(rb_recv[j, 16:32, :].astype(F32)[:, 16 * p : 16 * p + 16])
            val = jnp.concatenate(parts, axis=1)
            scale = lax.rsqrt(jnp.mean(val * val, axis=1, keepdims=True) + 1e-06)
            norm_out[16 * p : 16 * p + 16, :] = (val * scale * gain).astype(BF16)
        put(norm_out, norm_hbm, 1)

    def drain():
        for cp in written:
            cp.wait()
        for cp in sent:
            cp.wait_send()
        for p in range(PH):
            arrived(hs.at[p, pl.ds(0, 240)], tok_s.at[p])
        arrived(cot_mid.at[pl.ds(0, 3)], cot_s.at[0])
        arrived(cot_recv.at[pl.ds(0, 12)], cot_s.at[1])
        for i, ref in enumerate((sa_recv, sb_recv, ra_recv, rb_recv)):
            arrived(ref.at[pl.ds(0, 15)], all_s.at[i])

    def to_peer(o, src, dst, i):
        yy, ww = peer(o)
        return pltpu.make_async_remote_copy(
            src_ref=src(yy, ww), dst_ref=dst, send_sem=all_s.at[i], recv_sem=all_r.at[i],
            device_id=dev(yy, ww), device_id_type=MESH,
        )

    def sa_copy(o):
        return to_peer(o, lambda yy, ww: sa_send, sa_recv.at[mj], 0)

    def sb_copy(o):
        return to_peer(o, lambda yy, ww: sb_send, sb_recv.at[mj], 1)

    def ra_copy(o):
        return to_peer(o, lambda yy, ww: ra_send.at[ww * 4 + yy], ra_recv.at[mj], 2)

    def rb_copy(o):
        return to_peer(o, lambda yy, ww: rb_send.at[ww * 4 + yy], rb_recv.at[mj], 3)

    def got_all(ref, i):
        arrived(ref.at[pl.ds(0, 15)], all_r.at[i])

    def start_all(copy):
        @pl.loop(1, 16)
        def _(o):
            copy(o).start()

    def project(p):
        got_y(p)
        prod = lax.dot_general(
            wp[...].reshape(2 * PAD, HID), hs[p], (((1,), (1,)), ((), ())),
            preferred_element_type=F32,
        )
        val = jnp.concatenate([prod[0:ROWS], prod[PAD : PAD + ROWS]], axis=0)
        y_keep[p] = val.astype(BF16).astype(F32)

    def pack_a():
        for p in range(2):
            val = y_keep[p]
            ra_send[:, 16 * p : 16 * p + 16, :] = val[0:128].T.astype(BF16).reshape(16, 16, 128)
        ra_recv[mj] = ra_send[me]

    def pack_b():
        val = y_keep[2]
        rb_send[:, 0:16, :] = val[0:128].T.astype(BF16).reshape(16, 16, 128)
        ext = [y_keep[p][128:144] for p in range(PH)]
        ext = jnp.concatenate(ext + [jnp.zeros((80, TK), F32)], axis=0)
        rb_send[:, 16:32, :] = ext.T.astype(BF16).reshape(16, 16, 128)
        rb_recv[mj] = rb_send[me]

    def sums(p):
        val = y_keep[p]
        square = jnp.sum(val * val, axis=0, keepdims=True)
        cross = jnp.sum(val * a_keep[p], axis=0, keepdims=True)
        return jnp.concatenate([square, cross], axis=0)

    def weights(p, tot, last=False):
        scale = lax.rsqrt(tot[0:1] / D + 1e-06)
        cross = tot[1:2] / D
        dy = (scale * (a_keep[p] - y_keep[p] * (scale * scale * cross))).astype(BF16)
        for k in range(NCH):
            cols = pl.ds(k * CH, CH)
            add = jnp.dot(dy, hs[p, :, cols], preferred_element_type=F32)
            if p == 0:
                grad[:, cols] = add
            else:
                grad[:, cols] += add
            if last:
                other = pl.ds(pl.multiple_of((1 - c) * ROWS, 8), ROWS)
                send(grad.at[other, cols], grad_in.at[:, cols], g_s.at[k], g_r.at[k], twin)

    own_z(0)
    own(0)
    own_z(1)
    own(1)
    own(2)
    outer_x()
    share_w()
    pack_cot()
    cot_y()
    relay_y(0, 0)
    own_z(2)
    relay_y(1, 0)
    relay_y(2, 0)
    relay_z(0)
    spread(0, 1)
    spread(0, 2)
    outer_z()
    relay_y(0, 1)
    relay_y(0, 2)
    relay_z(1)
    spread(1, 1)
    spread(1, 2)
    relay_y(1, 1)
    relay_y(1, 2)
    relay_z(2)
    spread(2, 1)
    spread(2, 2)
    finish_z(0)
    relay_y(2, 1)
    relay_y(2, 2)
    relay_last(0)
    finish_z(1)
    cot_z()
    relay_last(1)
    ready()
    project(0)
    finish_z(2)
    relay_last(2)
    project(1)
    outer_back()
    get_cot()
    sums_a()
    start_all(sa_copy)
    pack_a()
    start_all(ra_copy)
    outer_step()
    project(2)
    sums_b()
    start_all(sb_copy)
    pack_b()
    start_all(rb_copy)
    weights_a()
    moments()
    get_b()
    weights_b()
    for k in range(NCH):
        swapped(k)
        adam(k)
    get_ret()
    norm_rows()
    drain()


def place_body(a_in, b_in, c_in, a_out, b_out, c_out, a, b, c, sem):
    stages = ((a_in, a, a_out), (b_in, b, b_out), (c_in, c, c_out))
    loads = [pltpu.make_async_copy(src, mid, sem.at[i]) for i, (src, mid, _) in enumerate(stages)]
    stores = [pltpu.make_async_copy(mid, dst, sem.at[3 + i]) for i, (_, mid, dst) in enumerate(stages)]
    for cp in loads:
        cp.start()
    for load, store in zip(loads, stores):
        load.wait()
        store.start()
    for cp in stores:
        cp.wait()


def place(*arrays):
    hbm = pl.BlockSpec(memory_space=pl.ANY)
    return pl.pallas_call(
        place_body,
        out_shape=tuple(jax.ShapeDtypeStruct(a.shape, a.dtype) for a in arrays),
        in_specs=[hbm] * 3,
        out_specs=(hbm,) * 3,
        scratch_shapes=[pltpu.VMEM(a.shape, a.dtype) for a in arrays] + [pltpu.SemaphoreType.DMA((6,))],
        compiler_params=pltpu.CompilerParams(vmem_limit_bytes=63 << 20),
    )(*arrays)


def per_device(hidden, down_w, m1, m2, gain, cot, delta, outer_params, outer_momentum):
    hbm = pl.BlockSpec(memory_space=pl.ANY)
    dma = pltpu.SemaphoreType.DMA
    scratch = [
        pltpu.VMEM((48, D), BF16),
        pltpu.VMEM((ROWS, HID), BF16),
        pltpu.VMEM((ROWS, 1024), F32),
        pltpu.VMEM((D,), BF16),
        pltpu.VMEM((PH, TK, HID), BF16),
        pltpu.VMEM((2, PAD, HID), BF16),
        pltpu.VMEM((ROWS, HID), BF16),
        pltpu.VMEM((ROWS, HID), BF16),
        pltpu.VMEM((ROWS, HID), BF16),
        pltpu.VMEM((FEAT, HID), F32),
        pltpu.VMEM((ROWS, HID), F32),
        pltpu.VMEM((48, D), BF16),
        pltpu.VMEM((ROWS, 1024), BF16),
        pltpu.VMEM((16, 64, 128), BF16),
        pltpu.VMEM((4, 4, 64, 128), BF16),
        pltpu.VMEM((16, 64, 128), BF16),
        pltpu.VMEM((16, 8, 128), F32),
        pltpu.VMEM((2, 2 * TK), F32),
        pltpu.VMEM((16, 2, 2 * TK), F32),
        pltpu.VMEM((2, TK), F32),
        pltpu.VMEM((16, 2, TK), F32),
        pltpu.VMEM((PH, FEAT, TK), F32),
        pltpu.VMEM((PH, FEAT, TK), F32),
        pltpu.VMEM((16, 32, 128), BF16),
        pltpu.VMEM((16, 32, 128), BF16),
        pltpu.VMEM((16, 32, 128), BF16),
        pltpu.VMEM((16, 32, 128), BF16),
        pltpu.VMEM((4, ROWS, 256), F32),
        pltpu.VMEM((4, ROWS, 256), F32),
        pltpu.VMEM((PAD, 256), BF16),
        pltpu.VMEM((4, PAD, 256), BF16),
        pltpu.VMEM((ROWS, 256), F32),
        pltpu.VMEM((4, ROWS, 256), F32),
        pltpu.VMEM((ROWS, 1024), F32),
        pltpu.VMEM((ROWS, 1024), F32),
        dma((11,)), dma((2 + NCH,)),
        dma((PH,)), dma((PH, 2)), dma((PH, 2)), dma((PH, 3, 2)), dma((PH, 2)), dma((PH,)),
        dma((1,)), dma((1,)),
        dma((2,)), dma((2,)), dma((4,)), dma((4,)),
        dma((NCH,)), dma((NCH,)),
        dma((4,)), dma((4,)), dma((4,)), dma((4,)), dma((4,)), dma((4,)),
    ]
    normed, adam, outer = pl.pallas_call(
        body,
        out_shape=(
            jax.ShapeDtypeStruct((48, D), BF16),
            jax.ShapeDtypeStruct((ROWS, HID), BF16),
            jax.ShapeDtypeStruct((ROWS, 1024), F32),
        ),
        in_specs=[hbm] * 9,
        out_specs=(hbm, hbm, hbm),
        scratch_shapes=scratch,
        compiler_params=pltpu.CompilerParams(
            collective_id=0, has_side_effects=True, vmem_limit_bytes=63 << 20
        ),
        cost_estimate=pl.CostEstimate(flops=2 * 10**9, bytes_accessed=4 * 10**6, transcendentals=0),
    )(
        hidden, down_w[0], m1[0], m2[0], gain, cot, delta[0],
        outer_params, outer_momentum,
    )
    return place(normed, adam[None], outer)


def solution(mesh):
    placed = (
        P(("group", "fsdp"), None),
        P("group", "fsdp", None),
        P("group", "fsdp", None),
        P("group", "fsdp", None),
        P(),
        P(("group", "fsdp"), None),
        P("group", "fsdp", None),
        P("fsdp", None),
        P("fsdp", None),
    )
    return jax.shard_map(
        per_device,
        mesh=mesh,
        in_specs=placed,
        out_specs=(P(("group", "fsdp"), None), P("group", "fsdp", None), P("fsdp", None)),
        check_vma=False,
    )
```

time: 446 us -> 121 us (0.27); the launches traced: 438 us -> 120 us
  waiting for transfers between devices: 379 us -> 0 us
  Pallas kernels: 0 us -> 120 us
  matrix products: 18.6 us -> 0 us
  starting transfers between devices: 17.9 us -> 0 us
  between operations: 15.6 us -> 0.64 us
    all_gather x1 -> x0, waiting for transfers between devices: 205 us -> none  [per_device(): gathered = lax.all_gather(hidden, 'fsdp', axis=0, tiled=True)]
    psum x1 -> x0, waiting for transfers between devices: 151 us -> none  [per_device(): lax.psum(frag_delta[0].astype(jnp.float32).astype(jnp.bfloat16), 'group')]
    pallas_call x0 -> x2, Pallas kernels: none -> 120 us  [the longest x1 118 us: per_device(): pl.pallas_call(body, out_shape=(jax.ShapeDtypeStruct((48, D), BF16), jax....]
    all_to_all x2 -> x0, waiting for transfers between devices: 22 us -> none  [the longest x1 22 us: per_device(): lax.all_to_all(columns, 'fsdp', split_axis=0, concat_axis=1, tiled=True)]
    dot_general x2 -> x0, matrix products: 18.6 us -> none  [the longest x1 9.47 us: per_device(): lax.dot_general(gathered, weight, (((1,), (1,)), ((), ())), preferred_ele...]
    all_to_all x2 -> x0, starting transfers between devices: 17.8 us -> none  [the longest x1 10.3 us: per_device(): lax.all_to_all(columns, 'fsdp', split_axis=0, concat_axis=1, tiled=True)]
  transfers between devices with their start and end apart: 4 -> 0, of which waited for: 3 -> 0; matrix products, arithmetic and copies ran while one was open for 0% -> 0% of each run, Pallas kernels for 0% -> 0%
where the time goes in v2:
time: 121 us; the launch traced here: 120 us
  Pallas kernels  120 us (99%)
    pallas_call x1, Pallas kernels, per_device(): pl.pallas_call(body, out_shape=(jax.ShapeDtypeStruct((48, D), BF16), jax....  118 us

profile of v2, /device:TPU:1, one launch (start us, length us, event | category | flops | bytes accessed | tf_op | source)
XLA Modules:
  0.0 120.4 jit_solution(9694003631837410323)
XLA Ops:
  0.6 117.6 %shard_map.112 = (bf16[48,2304]{1,0:T(8,128)(2,1)}, bf16[72,4608]{1,0:T(8,128)(2,1)}, f32[72,1024]{1,0:T(8,128)}) custom-call(bf16[48,4608]{1,0:T(8,128)(2,1)} %h_in.1, bf16[72,4608]{1,0:T(8,128)(2,1)} %bitcast.6, bf16[72,4608]{1,0:T(8,128)(2,1)} %bitcast.7, bf16[72,4608]{1,0:T(8,128)(2,1)} %bitcast.8, bf16[2304]{0:T(1024)(128)(2,1)} %gain_in.1, ...), custom_call_target="tpu_custom_call" | custom-call | flops 2000000000 | bytes 4000000 | tf_op jit(solution)/shard_map/pallas_call | solution.py:528
  118.2 2.2 %shard_map.113 = (bf16[48,2304]{1,0:T(8,128)(2,1)}, bf16[1,72,4608]{2,1,0:T(8,128)(2,1)}, f32[72,1024]{1,0:T(8,128)}) custom-call(bf16[48,2304]{1,0:T(8,128)(2,1)} %get-tuple-element.6.a_in, bf16[1,72,4608]{2,1,0:T(8,128)(2,1)} %bitcast.5, f32[72,1024]{1,0:T(8,128)} %get-tuple-element.8.c_in), custom_call_target="tpu_custom_call" | custom-call | tf_op jit(solution)/shard_map/pallas_call | solution.py:472

commit v3 on v2

--- a/solution.py
+++ b/solution.py
@@ -16,7 +16,7 @@
 PAD = 80
 PH = 3
 TK = 256
-CH = 1152
+CH = 1536
 NCH = HID // CH
 
 
@@ -24,12 +24,12 @@
     h_in, w_in, m1_in, m2_in, gain_in, cot_in, delta_in, op_in, om_in,
     norm_hbm, adam_hbm, outer_hbm,
     norm_out, adam_out, outer_out, gain_v,
-    hs, wp, w_own, m1, m2, grad, grad_in, cot, delta,
-    cot_send, cot_mid, cot_recv, gain_rows, sa_send, sa_recv, sb_send, sb_recv, a_keep, y_keep,
+    hs, wp, wt, w_own, m1, m2, grad, grad_in, cot, delta,
+    cot_send, cot_mid, cot_recv, gain_rows, st_send, st_mid, st_y, st_z, a_keep, y_keep,
     ra_send, ra_recv, rb_send, rb_recv,
     d_own, d_recv, z_send, z_recv, o_own, o_recv, op, om,
     loc, out_sem, tok_s, zs_r, zx_r, ys_r, yh_r, yx_r,
-    w_s, w_r, cot_s, cot_r, all_s, all_r, g_s, g_r,
+    w_s, w_r, cot_s, cot_r, st_s, st_r, all_s, all_r, g_s, g_r,
     dx_s, dx_r, dz_s, dz_r, do_s, do_r,
 ):
     g = lax.axis_index("group")
@@ -158,7 +158,7 @@
     def cot_z():
         arrived(cot_mid.at[pl.ds(0, 3)], cot_r.at[0])
         here = pl.ds(pl.multiple_of(w * 4, 4), 4)
-        for k in (1, 3, 2):
+        for k in (2, 1, 3):
             ww = mod4(w + k)
             send(cot_mid.at[:, ww], cot_recv.at[here], cot_s.at[1], cot_r.at[1], dev(y, ww), False)
         cot_recv[here] = cot_mid[:, w]
@@ -233,6 +233,10 @@
 
     def ready():
         arrived(wp.at[1 - c], w_r.at[0])
+        for k in range(NCH):
+            cols = pl.ds(k * CH, CH)
+            part = wp[:, :, cols].reshape(2 * PAD, CH).astype(F32).T
+            wt[cols, :] = part.astype(BF16)
         local[3].wait()
         local[4].wait()
         local[5].wait()
@@ -248,30 +252,18 @@
         ext_all = cot_recv[:, 48:64, :].reshape(TK, 128).astype(F32).T
         for p in range(PH):
             main = cot_recv[:, 16 * p : 16 * p + 16, :].reshape(TK, 128).astype(F32).T
-            a_keep[p] = gcol * jnp.concatenate([main, ext_all[16 * p : 16 * p + 16]], axis=0)
-
-    def sums_a():
-        both = jnp.concatenate([sums(0), sums(1)], axis=1)
-        sa_send[...] = both
-        sa_recv[mj] = both
-
-    def sums_b():
-        both = sums(2)
-        sb_send[...] = both
-        sb_recv[mj] = both
-
-    def weights_a():
-        got_all(sa_recv, 0)
-
-        tot = jnp.sum(sa_recv[...], axis=0)
-        weights(0, tot[:, 0:TK])
-        weights(1, tot[:, TK : 2 * TK])
-
-    def get_b():
-        got_all(sb_recv, 1)
-
-    def weights_b():
-        weights(2, jnp.sum(sb_recv[...], axis=0), last=True)
+            a_keep[:, TK * p : TK * (p + 1)] = gcol * jnp.concatenate([main, ext_all[16 * p : 16 * p + 16]], axis=0)
+
+    def sums_y():
+        arrived(st_y.at[pl.ds(0, 3)], st_r.at[0])
+        both = jnp.sum(st_y[...], axis=0)
+        st_mid[...] = both
+        st_z[w] = both
+        for k in (2, 1, 3):
+            send(st_mid, st_z.at[w], st_s.at[1], st_r.at[1], dev(y, mod4(w + k)), False)
+
+    def get_stats():
+        arrived(st_z.at[pl.ds(0, 3)], st_r.at[1])
 
     def swapped(k):
         cols = pl.ds(k * CH, CH)
@@ -292,8 +284,8 @@
         local[7].wait()
 
     def get_ret():
-        got_all(ra_recv, 2)
-        got_all(rb_recv, 3)
+        got_all(ra_recv, 0)
+        got_all(rb_recv, 1)
 
     def norm_rows():
         gain = gain_v[...].reshape(1, D).astype(F32)
@@ -317,7 +309,9 @@
             arrived(hs.at[p, pl.ds(0, 240)], tok_s.at[p])
         arrived(cot_mid.at[pl.ds(0, 3)], cot_s.at[0])
         arrived(cot_recv.at[pl.ds(0, 12)], cot_s.at[1])
-        for i, ref in enumerate((sa_recv, sb_recv, ra_recv, rb_recv)):
+        for i in range(2):
+            arrived(st_y.at[pl.ds(0, 3)], st_s.at[i])
+        for i, ref in enumerate((ra_recv, rb_recv)):
             arrived(ref.at[pl.ds(0, 15)], all_s.at[i])
 
     def to_peer(o, src, dst, i):
@@ -327,17 +321,11 @@
             device_id=dev(yy, ww), device_id_type=MESH,
         )
 
-    def sa_copy(o):
-        return to_peer(o, lambda yy, ww: sa_send, sa_recv.at[mj], 0)
-
-    def sb_copy(o):
-        return to_peer(o, lambda yy, ww: sb_send, sb_recv.at[mj], 1)
-
     def ra_copy(o):
-        return to_peer(o, lambda yy, ww: ra_send.at[ww * 4 + yy], ra_recv.at[mj], 2)
+        return to_peer(o, lambda yy, ww: ra_send.at[ww * 4 + yy], ra_recv.at[mj], 0)
 
     def rb_copy(o):
-        return to_peer(o, lambda yy, ww: rb_send.at[ww * 4 + yy], rb_recv.at[mj], 3)
+        return to_peer(o, lambda yy, ww: rb_send.at[ww * 4 + yy], rb_recv.at[mj], 1)
 
     def got_all(ref, i):
         arrived(ref.at[pl.ds(0, 15)], all_r.at[i])
@@ -349,47 +337,46 @@
 
     def project(p):
         got_y(p)
-        prod = lax.dot_general(
-            wp[...].reshape(2 * PAD, HID), hs[p], (((1,), (1,)), ((), ())),
-            preferred_element_type=F32,
-        )
+        prod = jnp.dot(hs[p], wt[...], preferred_element_type=F32).T
         val = jnp.concatenate([prod[0:ROWS], prod[PAD : PAD + ROWS]], axis=0)
-        y_keep[p] = val.astype(BF16).astype(F32)
+        y_keep[:, TK * p : TK * (p + 1)] = val.astype(BF16).astype(F32)
 
     def pack_a():
         for p in range(2):
-            val = y_keep[p]
+            val = y_keep[:, TK * p : TK * (p + 1)]
             ra_send[:, 16 * p : 16 * p + 16, :] = val[0:128].T.astype(BF16).reshape(16, 16, 128)
         ra_recv[mj] = ra_send[me]
 
     def pack_b():
-        val = y_keep[2]
+        val = y_keep[:, 2 * TK :]
         rb_send[:, 0:16, :] = val[0:128].T.astype(BF16).reshape(16, 16, 128)
-        ext = [y_keep[p][128:144] for p in range(PH)]
+        ext = [y_keep[128:144, TK * p : TK * (p + 1)] for p in range(PH)]
         ext = jnp.concatenate(ext + [jnp.zeros((80, TK), F32)], axis=0)
         rb_send[:, 16:32, :] = ext.T.astype(BF16).reshape(16, 16, 128)
         rb_recv[mj] = rb_send[me]
 
-    def sums(p):
-        val = y_keep[p]
+    def sums():
+        val = y_keep[...]
         square = jnp.sum(val * val, axis=0, keepdims=True)
-        cross = jnp.sum(val * a_keep[p], axis=0, keepdims=True)
-        return jnp.concatenate([square, cross], axis=0)
-
-    def weights(p, tot, last=False):
+        cross = jnp.sum(val * a_keep[...], axis=0, keepdims=True)
+        both = jnp.concatenate([square, cross], axis=0)
+        st_send[...] = both
+        st_y[y] = both
+        for k in range(1, 4):
+            send(st_send, st_y.at[y], st_s.at[0], st_r.at[0], dev(mod4(y + k), w), False)
+
+    def weights():
+        tot = jnp.sum(st_z[...], axis=0)
         scale = lax.rsqrt(tot[0:1] / D + 1e-06)
         cross = tot[1:2] / D
-        dy = (scale * (a_keep[p] - y_keep[p] * (scale * scale * cross))).astype(BF16)
+        dy = (scale * (a_keep[...] - y_keep[...] * (scale * scale * cross))).astype(BF16)
+        other = pl.ds(pl.multiple_of((1 - c) * ROWS, 8), ROWS)
         for k in range(NCH):
             cols = pl.ds(k * CH, CH)
-            add = jnp.dot(dy, hs[p, :, cols], preferred_element_type=F32)
-            if p == 0:
-                grad[:, cols] = add
-            else:
-                grad[:, cols] += add
-            if last:
-                other = pl.ds(pl.multiple_of((1 - c) * ROWS, 8), ROWS)
-                send(grad.at[other, cols], grad_in.at[:, cols], g_s.at[k], g_r.at[k], twin)
+            grad[:, cols] = jnp.dot(
+                dy, hs[:, :, cols].reshape(PH * TK, CH), preferred_element_type=F32
+            )
+            send(grad.at[other, cols], grad_in.at[:, cols], g_s.at[k], g_r.at[k], twin)
 
     own_z(0)
     own(0)
@@ -414,38 +401,35 @@
     spread(1, 1)
     spread(1, 2)
     relay_y(1, 1)
-    relay_y(1, 2)
     relay_z(2)
     spread(2, 1)
     spread(2, 2)
+    relay_y(1, 2)
     finish_z(0)
     relay_y(2, 1)
     relay_y(2, 2)
     relay_last(0)
+    ready()
     finish_z(1)
     cot_z()
+    finish_z(2)
     relay_last(1)
-    ready()
+    outer_back()
     project(0)
-    finish_z(2)
     relay_last(2)
     project(1)
-    outer_back()
-    get_cot()
-    sums_a()
-    start_all(sa_copy)
     pack_a()
     start_all(ra_copy)
+    get_cot()
+    project(2)
+    sums()
+    pack_b()
+    moments()
     outer_step()
-    project(2)
-    sums_b()
-    start_all(sb_copy)
-    pack_b()
+    sums_y()
     start_all(rb_copy)
-    weights_a()
-    moments()
-    get_b()
-    weights_b()
+    get_stats()
+    weights()
     for k in range(NCH):
         swapped(k)
         adam(k)
@@ -489,6 +473,7 @@
         pltpu.VMEM((D,), BF16),
         pltpu.VMEM((PH, TK, HID), BF16),
         pltpu.VMEM((2, PAD, HID), BF16),
+        pltpu.VMEM((HID, 2 * PAD), BF16),
         pltpu.VMEM((ROWS, HID), BF16),
         pltpu.VMEM((ROWS, HID), BF16),
         pltpu.VMEM((ROWS, HID), BF16),
@@ -500,12 +485,12 @@
         pltpu.VMEM((4, 4, 64, 128), BF16),
         pltpu.VMEM((16, 64, 128), BF16),
         pltpu.VMEM((16, 8, 128), F32),
-        pltpu.VMEM((2, 2 * TK), F32),
-        pltpu.VMEM((16, 2, 2 * TK), F32),
-        pltpu.VMEM((2, TK), F32),
-        pltpu.VMEM((16, 2, TK), F32),
-        pltpu.VMEM((PH, FEAT, TK), F32),
-        pltpu.VMEM((PH, FEAT, TK), F32),
+        pltpu.VMEM((2, PH * TK), F32),
+        pltpu.VMEM((2, PH * TK), F32),
+        pltpu.VMEM((4, 2, PH * TK), F32),
+        pltpu.VMEM((4, 2, PH * TK), F32),
+        pltpu.VMEM((FEAT, PH * TK), F32),
+        pltpu.VMEM((FEAT, PH * TK), F32),
         pltpu.VMEM((16, 32, 128), BF16),
         pltpu.VMEM((16, 32, 128), BF16),
         pltpu.VMEM((16, 32, 128), BF16),
@@ -521,7 +506,7 @@
         dma((11,)), dma((2 + NCH,)),
         dma((PH,)), dma((PH, 2)), dma((PH, 2)), dma((PH, 3, 2)), dma((PH, 2)), dma((PH,)),
         dma((1,)), dma((1,)),
-        dma((2,)), dma((2,)), dma((4,)), dma((4,)),
+        dma((2,)), dma((2,)), dma((2,)), dma((2,)), dma((2,)), dma((2,)),
         dma((NCH,)), dma((NCH,)),
         dma((4,)), dma((4,)), dma((4,)), dma((4,)), dma((4,)), dma((4,)),
     ]

time: 121 us -> 116 us (0.959)
  Pallas kernels: 120 us -> 115 us
    pallas_call x1, Pallas kernels: 118 us -> 113 us  [per_device(): pl.pallas_call(body, out_shape=(jax.ShapeDtypeStruct((48, D), BF16), jax....]
where the time goes in v3:
time: 116 us
  Pallas kernels  115 us (99%)
    pallas_call x1, Pallas kernels, per_device(): pl.pallas_call(body, out_shape=(jax.ShapeDtypeStruct((48, D), BF16), jax....  113 us

profile of v3, /device:TPU:1, one launch (start us, length us, event | category | flops | bytes accessed | tf_op | source)
XLA Modules:
  0.0 116.1 jit_solution(1630833249257108927)
XLA Ops:
  0.6 113.3 %shard_map.112 = (bf16[48,2304]{1,0:T(8,128)(2,1)}, bf16[72,4608]{1,0:T(8,128)(2,1)}, f32[72,1024]{1,0:T(8,128)}) custom-call(bf16[48,4608]{1,0:T(8,128)(2,1)} %h_in.1, bf16[72,4608]{1,0:T(8,128)(2,1)} %bitcast.6, bf16[72,4608]{1,0:T(8,128)(2,1)} %bitcast.7, bf16[72,4608]{1,0:T(8,128)(2,1)} %bitcast.8, bf16[2304]{0:T(1024)(128)(2,1)} %gain_in.1, ...), custom_call_target="tpu_custom_call" | custom-call | flops 2000000000 | bytes 4000000 | tf_op jit(solution)/shard_map/pallas_call | solution.py:513
  113.9 2.2 %shard_map.113 = (bf16[48,2304]{1,0:T(8,128)(2,1)}, bf16[1,72,4608]{2,1,0:T(8,128)(2,1)}, f32[72,1024]{1,0:T(8,128)}) custom-call(bf16[48,2304]{1,0:T(8,128)(2,1)} %get-tuple-element.6.a_in, bf16[1,72,4608]{2,1,0:T(8,128)(2,1)} %bitcast.5, f32[72,1024]{1,0:T(8,128)} %get-tuple-element.8.c_in), custom_call_target="tpu_custom_call" | custom-call | tf_op jit(solution)/shard_map/pallas_call | solution.py:456
